TPU v7x, 256 devices: a whole 4x4x8 slice. The times are simulated.
256 devices in a mesh: ctx: 32 (over y, x, z_lo), ch: 8 (over z_hi, core).
Axes of the slice: x: 4, y: 4, z: 8 (z_hi: 4, z_lo: 2; z = z_hi * 2 + z_lo), core: 2. Of those that a mesh axis runs over, the one named last changes fastest.
Arguments:
- tokens: bfloat16 [65536, 1024], P('ctx', 'ch'), may hold values from -6 to 6
- w_in: bfloat16 [1024, 1024], P(None, 'ch'), may hold values from -0.1875 to 0.1875
- filters: float32 [65536, 24], P('ctx'), may hold values from -0.0234375 to 0.0234375
- w_filter: float32 [24, 1024], P(None, 'ch'), may hold values from -1.25 to 1.25
- w_out: bfloat16 [1024, 1024], P('ch'), may hold values from -0.1875 to 0.1875
Outputs:
- output: bfloat16 [65536, 1024], P('ctx', 'ch')
All inputs are finite; a program needn't handle non-finite values.
Results may differ from a plain program's by a relative error of at most 0.0049.
Values may be sent and summed in bfloat16 or wider, within the bound.
No kernel may reach another device: no remote copies, remote signals or barrier semaphores. Data moves between devices by JAX's collectives and lax.ppermute only.
A program may use at most 64 MiB of HBM per device.

v0:
```python
import math
import jax
import jax.numpy as jnp
from jax import lax
from jax.sharding import PartitionSpec as P

COLS = 256
highest_mode = lax.Precision.HIGHEST


def cos_sin_table(left_index, right_index, period):
    phases = left_index[:, None] * right_index[None, :] % period
    angles = 2.0 * math.pi / period * phases.astype(jnp.float32)
    return (jnp.cos(angles), jnp.sin(angles))


def local(tokens, w_in, filters, w_filter, w_out):
    row_count, chan_count = tokens.shape
    ctx_count = lax.axis_size("ctx")
    ctx_place = lax.axis_index("ctx")
    inner_len = COLS
    outer_dev = row_count // inner_len
    outer_len = outer_dev * ctx_count
    padded_len = 2 * outer_len
    total_len = padded_len * inner_len
    inner_dev = inner_len // ctx_count
    projected = jnp.dot(
        lax.all_gather(tokens, "ch", axis=1, tiled=True), w_in, preferred_element_type=jnp.float32
    )
    shaped = jnp.dot(filters, w_filter, precision=highest_mode)
    signal = jnp.concatenate([projected, shaped], axis=1)
    signal = signal.reshape(outer_dev, inner_len, signal.shape[1])
    outer_index = jnp.arange(outer_len, dtype=jnp.int32)
    padded_index = jnp.arange(padded_len, dtype=jnp.int32)
    inner_index = jnp.arange(inner_len, dtype=jnp.int32)
    local_inner = ctx_place * inner_dev + jnp.arange(inner_dev, dtype=jnp.int32)
    outer_cos, outer_sin = cos_sin_table(padded_index, outer_index, padded_len)
    twiddle_cos, twiddle_sin = cos_sin_table(padded_index, local_inner, total_len)
    twiddle_cos = twiddle_cos[:, :, None]
    twiddle_sin = twiddle_sin[:, :, None]
    inner_cos, inner_sin = cos_sin_table(inner_index, inner_index, inner_len)
    block_part = lax.all_to_all(signal, "ctx", split_axis=1, concat_axis=0, tiled=True)
    real_part = jnp.einsum("kn,nbc->kbc", outer_cos, block_part, precision=highest_mode)
    imag_part = -jnp.einsum("kn,nbc->kbc", outer_sin, block_part, precision=highest_mode)
    first_spectra = jnp.stack(
        [
            real_part * twiddle_cos + imag_part * twiddle_sin,
            imag_part * twiddle_cos - real_part * twiddle_sin,
        ]
    )

    def inner_product(table, values):
        return jnp.einsum("kn,fnc->fkc", table, values, precision=highest_mode)

    block_part = lax.all_to_all(first_spectra, "ctx", split_axis=1, concat_axis=2, tiled=True)
    real_in = block_part[0]
    imag_in = block_part[1]
    real_out = inner_product(inner_cos, real_in) + inner_product(inner_sin, imag_in)
    imag_out = inner_product(inner_cos, imag_in) - inner_product(inner_sin, real_in)
    spectra = jnp.stack([real_out, imag_out])
    signal_re = spectra[0, :, :, :chan_count]
    signal_im = spectra[1, :, :, :chan_count]
    kernel = spectra[:, :, :, chan_count:]
    product_re = signal_re * kernel[0] - signal_im * kernel[1]
    product_im = signal_re * kernel[1] + signal_im * kernel[0]
    back_re = inner_product(inner_cos, product_re) - inner_product(inner_sin, product_im)
    back_im = inner_product(inner_cos, product_im) + inner_product(inner_sin, product_re)
    halfway = jnp.stack([back_re, back_im])
    block_part = lax.all_to_all(halfway, "ctx", split_axis=2, concat_axis=1, tiled=True)
    real_in = block_part[0]
    imag_in = block_part[1]
    turned_re = real_in * twiddle_cos - imag_in * twiddle_sin
    turned_im = imag_in * twiddle_cos + real_in * twiddle_sin
    summed = jnp.einsum("kn,kbc->nbc", outer_cos, turned_re, precision=highest_mode)
    summed = summed - jnp.einsum("kn,kbc->nbc", outer_sin, turned_im, precision=highest_mode)
    positions = summed * (1.0 / total_len)
    conv = (
        lax.all_to_all(
            positions.astype(jnp.bfloat16), "ctx", split_axis=0, concat_axis=1, tiled=True
        )
        .astype(positions.dtype)
        .reshape(row_count, chan_count)
    )
    mixed = conv.astype(jnp.bfloat16)
    partial_terms = jnp.dot(mixed, w_out, preferred_element_type=jnp.float32)
    result = lax.psum_scatter(partial_terms, "ch", scatter_dimension=1, tiled=True)
    return result.astype(jnp.bfloat16)


def solution(mesh):
    placed = (P("ctx", "ch"), P(None, "ch"), P("ctx", None), P(None, "ch"), P("ch", None))
    return jax.shard_map(
        local, mesh=mesh, in_specs=placed, out_specs=P("ctx", "ch"), check_vma=False
    )
```

profile of v0, /device:TPU:40, one launch (start us, length us, event | category | flops | bytes accessed | tf_op | source)
XLA Modules:
  0.0 496.1 jit_solution(14305966484975328182)
XLA Ops:
  6.5 0.0 all-gather.2.cloned.1.call-start
  6.5 0.7 all-gather.2.cloned.1.call-update
  7.3 1.9 fusion.152
  9.2 57.7 %all-gather.2.cloned.1.call-done = bf16[2048,1024]{1,0:T(8,128)(2,1)} async-done(((bf16[2048,128]{1,0:T(8,128)(2,1)}), bf16[2048,1024]{1,0:T(8,128)(2,1)}) %all-gather.2.cloned.1.call-update) | async-done | bytes 4194320 | tf_op jit(solution)/shard_map/all_gather | solution.py:28
  66.9 3.7 fusion.151
  70.6 0.1 pad_maximum_fusion.2
  70.8 0.9 copy.92
  71.7 2.1 copy.60
  73.7 9.4 %all-to-all-start = ((f32[8,256,256]{2,0,1:T(8,128)}), f32[8,256,256]{2,0,1:T(8,128)S(1)}, u32[]{:S(2)}, u32[]{:S(2)}) async-start(f32[8,256,256]{2,0,1:T(8,128)} %copy.60), calls=%async_computation | async-start | bytes 4194304 | tf_op jit(solution)/shard_map/all_to_all | solution.py:42
  83.2 0.2 fusion.96
  83.3 27.2 %all-to-all-done = f32[8,256,256]{2,0,1:T(8,128)S(1)} async-done(((f32[8,256,256]{2,0,1:T(8,128)}), f32[8,256,256]{2,0,1:T(8,128)S(1)}, u32[]{:S(2)}, u32[]{:S(2)}) %all-to-all-start) | async-done | bytes 2097184 | tf_op jit(solution)/shard_map/all_to_all | solution.py:42
  110.5 5.8 %fusion.26 = f32[512,8,256]{2,0,1:T(8,128)S(1)} fusion(f32[32,8,8,256]{3,1,2,0:T(8,128)S(1)} %bitcast.127), kind=kOutput, calls=%fused_computation.34 | convolution fusion | flops 3223060480 | bytes 6291456 | tf_op jit(solution)/shard_map/kn,nbc->kbc/dot_general | solution.py:44
  116.3 20.1 %add_bitcast_fusion.1 = (f32[1,512,8,256]{3,1,2,0:T(8,128)S(1)}, f32[1,512,8,256]{3,1,2,0:T(8,128)S(1)}) fusion(f32[512,8,256]{2,0,1:T(8,128)S(1)} %fusion.26, f32[512,8]{0,1:T(8,128)S(1)} %get-tuple-element.16, f32[512,8]{0,1:T(8,128)S(1)} %get-tuple-element.15, f32[32,8,8,256]{3,1,2,0:T(8,128)S(1)} %bitcast.128), kind=kOutput, calls=%fused_computation.14 | convolution fusion | flops 3230400512 | bytes 14712832 | tf_op jit(solution)/shard_map/kn,nbc->kbc/dot_general | solution.py:43
  136.4 0.7 pad_maximum_fusion
  137.1 4.9 copy.65
  142.0 100.5 %all_to_all.66 = f32[2,512,8,256]{3,2,0,1:T(8,128)S(1)} all-to-all(f32[2,512,8,256]{3,2,0,1:T(8,128)S(1)} %copy.65), channel_id=1, replica_groups=mesh['ctx'=32,'ch'=8] {'ctx'}, dimensions={1} | all-to-all | bytes 16777216 | tf_op jit(solution)/shard_map/all_to_all | solution.py:55
  242.5 0.7 copy.66
  243.2 1.0 fusion.145
  244.2 7.9 %fusion.2 = f32[16,256,256]{2,1,0:T(8,128)S(1)} fusion(f32[1,16,32,8,256]{4,3,1,2,0:T(8,128)S(1)} %get-tuple-element.10), kind=kOutput, calls=%fused_computation.4 | convolution fusion | flops 3222142976 | bytes 8388608 | tf_op jit(solution)/shard_map/kn,fnc->fkc/dot_general | solution.py:53
  252.1 8.4 %fusion = f32[16,256,256]{2,1,0:T(8,128)S(1)} fusion(f32[1,16,32,8,256]{4,3,1,2,0:T(8,128)S(1)} %get-tuple-element.10), kind=kOutput, calls=%fused_computation.2 | convolution fusion | flops 3222142976 | bytes 8388608 | tf_op jit(solution)/shard_map/kn,fnc->fkc/dot_general | solution.py:53
  260.5 8.3 %add_bitcast_fusion = f32[1,16,256,256]{2,3,1,0:T(8,128)S(1)} fusion(f32[16,256,256]{2,1,0:T(8,128)S(1)} %fusion.2, f32[1,16,32,8,256]{4,3,1,2,0:T(8,128)S(1)} %get-tuple-element.9), kind=kOutput, calls=%fused_computation.12 | convolution fusion | flops 3223191552 | bytes 12582912 | tf_op jit(solution)/shard_map/kn,fnc->fkc/dot_general | solution.py:53
  268.8 8.3 %subtract_bitcast_fusion = f32[1,16,256,256]{2,3,1,0:T(8,128)S(1)} fusion(f32[16,256,256]{2,1,0:T(8,128)S(1)} %fusion, f32[1,16,32,8,256]{4,3,1,2,0:T(8,128)S(1)} %get-tuple-element.9), kind=kOutput, calls=%fused_computation.11 | convolution fusion | flops 3223191552 | bytes 12582912 | tf_op jit(solution)/shard_map/kn,fnc->fkc/dot_general | solution.py:53
  277.1 0.7 multiply_subtract_fusion
  277.8 2.8 fusion.20
  280.6 3.0 fusion.18
  283.7 2.9 subtract_bitcast_fusion.2
  286.6 2.9 add_bitcast_fusion.2
  289.4 2.3 pad_maximum_fusion.1
  291.8 5.5 %copy.73 = f32[2,16,256,128]{3,1,0,2:T(8,128)} copy(f32[2,16,256,128]{2,3,1,0:T(8,128)} %pad_maximum_fusion.1) | data formatting | bytes 8388608 | tf_op jit(solution)/shard_map/stack | solution.py:68
  297.2 7.2 %all-to-all-start.2 = ((f32[2,16,256,128]{3,1,0,2:T(8,128)}), f32[2,16,256,128]{3,1,0,2:T(8,128)}, u32[]{:S(2)}, u32[]{:S(2)}) async-start(f32[2,16,256,128]{3,1,0,2:T(8,128)} %copy.73), calls=%async_computation.2 | async-start | bytes 8388608 | tf_op jit(solution)/shard_map/all_to_all | solution.py:69
  304.4 0.3 reduce-scatter.2.cloned.1.call-start
  304.7 0.1 copy.76
  304.8 0.1 copy.78
  305.0 49.1 %all-to-all-done.2 = f32[2,16,256,128]{3,1,0,2:T(8,128)} async-done(((f32[2,16,256,128]{3,1,0,2:T(8,128)}), f32[2,16,256,128]{3,1,0,2:T(8,128)}, u32[]{:S(2)}, u32[]{:S(2)}) %all-to-all-start.2) | async-done | bytes 4194336 | tf_op jit(solution)/shard_map/all_to_all | solution.py:69
  354.1 4.6 copy.134
  358.7 0.4 fusion.146
  359.2 0.3 copy.75
  359.4 0.3 copy.77
  359.7 1.6 fusion.16
  361.3 3.9 fusion.30
  365.3 4.0 fusion.46
  369.3 0.3 copy.81
  369.6 15.6 %all_to_all.67 = bf16[256,8,128]{2,1,0:T(8,128)(2,1)S(1)} all-to-all(bf16[256,8,128]{2,1,0:T(8,128)(2,1)S(1)} %copy.81), channel_id=1, replica_groups=mesh['ctx'=32,'ch'=8] {'ctx'}, dimensions={0} | all-to-all | bytes 1048576 | tf_op jit(solution)/shard_map/all_to_all | solution.py:78
  385.3 0.1 copy.82
  385.4 4.5 fusion.153
  389.8 0.0 reduce-scatter.2.cloned.1.call-update
  389.9 96.9 %reduce-scatter.2.cloned.1.call-done = f32[2048,128]{1,0:T(8,128)} async-done(((f32[2048,1024]{1,0:T(8,128)}), f32[2048,128]{1,0:T(8,128)}) %reduce-scatter.2.cloned.1.call-update) | async-done | bytes 1048592 | tf_op jit(solution)/shard_map/reduce_scatter | solution.py:86
  486.8 2.1 convert_element_type.49
  (3 shorter events, 0.0 us)
Async XLA Ops:
  6.5 378.8 %copy-start = (bf16[128,1024]{1,0:T(8,128)(2,1)S(1)}, bf16[128,1024]{1,0:T(8,128)(2,1)}, u32[]{:S(2)}) copy-start(bf16[128,1024]{1,0:T(8,128)(2,1)} %param.9) | copy-start | bytes 786436
  6.5 60.4 %all-gather.2.cloned.1.call-start = ((), (), s32[]{:S(2)}) async-start(), calls=%async_computation.5 | async-start | bytes 4718592 | tf_op jit(solution)/shard_map/all_gather | solution.py:28
  73.7 36.8 %all-to-all-start = ((f32[8,256,256]{2,0,1:T(8,128)}), f32[8,256,256]{2,0,1:T(8,128)S(1)}, u32[]{:S(2)}, u32[]{:S(2)}) async-start(f32[8,256,256]{2,0,1:T(8,128)} %copy.60), calls=%async_computation | async-start | bytes 4194304 | tf_op jit(solution)/shard_map/all_to_all | solution.py:42
  297.2 56.9 %all-to-all-start.2 = ((f32[2,16,256,128]{3,1,0,2:T(8,128)}), f32[2,16,256,128]{3,1,0,2:T(8,128)}, u32[]{:S(2)}, u32[]{:S(2)}) async-start(f32[2,16,256,128]{3,1,0,2:T(8,128)} %copy.73), calls=%async_computation.2 | async-start | bytes 8388608 | tf_op jit(solution)/shard_map/all_to_all | solution.py:69
  304.4 182.4 %reduce-scatter.2.cloned.1.call-start = ((), (), s32[]{:S(2)}) async-start(), calls=%async_computation.6 | async-start | bytes 9437184 | tf_op jit(solution)/shard_map/reduce_scatter | solution.py:86
Sparse Core Ops, SparseCore 0:
  9.2 57.6 all-gather.1
  390.0 96.7 reduce-scatter.1
where the time goes:
time: 500 us; the launch traced here: 496 us
  waiting for transfers between devices  232 us (46%)
  blocking collectives  116 us (23%)
  matrix products  88.4 us (18%)
  local copies, waits for them, and re-layouts  21.2 us (4%)
  starting transfers between devices  16.9 us (3%)
  between operations  14.1 us (3%)
  other arithmetic  7.71 us (2%)
    all_to_all x1, blocking collectives, local(): lax.all_to_all(first_spectra, 'ctx', split_axis=1, concat_axis=2, tiled=T...  101 us
    reduce_scatter x1, waiting for transfers between devices, local(): lax.psum_scatter(partial_terms, 'ch', scatter_dimension=1, tiled=True)  96.9 us
    all_gather x1, waiting for transfers between devices, local(): lax.all_gather(tokens, 'ch', axis=1, tiled=True)  57.7 us
    all_to_all x1, waiting for transfers between devices, local(): lax.all_to_all(halfway, 'ctx', split_axis=2, concat_axis=1, tiled=True)  49.1 us
    dot_general x8, matrix products, inner_product(): return jnp.einsum('kn,fnc->fkc', table, values, precision=highest_mode)  44.5 us
    all_to_all x1, waiting for transfers between devices, local(): lax.all_to_all(signal, 'ctx', split_axis=1, concat_axis=0, tiled=True)  27.2 us
    dot_general x1, matrix products, local(): jnp.einsum('kn,nbc->kbc', outer_cos, block_part, precision=highest_mode)  20.1 us
    all_to_all x1, blocking collectives, local(): lax.all_to_all(positions.astype(jnp.bfloat16), 'ctx', split_axis=0, conca...  15.6 us
  transfers between devices with their start and end apart: 4, of which 4 were waited for; matrix products, arithmetic and copies ran while one was open for 0% of the time, Pallas kernels for 0%

commit v1 on v0

--- a/solution.py
+++ b/solution.py
@@ -6,6 +6,11 @@
 
 COLS = 256
 highest_mode = lax.Precision.HIGHEST
+
+
+def swapped_in(x, axis, dim):
+    sent = jnp.stack([x] * lax.axis_size(axis))
+    return jnp.concatenate(lax.all_to_all(sent, axis, 0, 0), axis=dim)
 
 
 def cos_sin_table(left_index, right_index, period):
@@ -24,9 +29,7 @@
     padded_len = 2 * outer_len
     total_len = padded_len * inner_len
     inner_dev = inner_len // ctx_count
-    projected = jnp.dot(
-        lax.all_gather(tokens, "ch", axis=1, tiled=True), w_in, preferred_element_type=jnp.float32
-    )
+    projected = jnp.dot(swapped_in(tokens, "ch", 1), w_in, preferred_element_type=jnp.float32)
     shaped = jnp.dot(filters, w_filter, precision=highest_mode)
     signal = jnp.concatenate([projected, shaped], axis=1)
     signal = signal.reshape(outer_dev, inner_len, signal.shape[1])

time: 500 us -> 542 us (1.084)
  waiting for transfers between devices: 232 us -> 266 us
  starting transfers between devices: 16.9 us -> 24 us
    all_to_all x0 -> x1, waiting for transfers between devices: none -> 95.7 us  [swapped_in(): return jnp.concatenate(lax.all_to_all(sent, axis, 0, 0), axis=dim)]
    all_gather x1 -> x0, waiting for transfers between devices: 57.7 us -> none  [local(): lax.all_gather(tokens, 'ch', axis=1, tiled=True)]
    all_to_all x0 -> x1, starting transfers between devices: none -> 7.7 us  [swapped_in(): return jnp.concatenate(lax.all_to_all(sent, axis, 0, 0), axis=dim)]
where the time goes in v1:
time: 542 us; the launch traced here: 538 us
  waiting for transfers between devices  266 us (49%)
  blocking collectives  114 us (21%)
  matrix products  86.7 us (16%)
  local copies, waits for them, and re-layouts  25 us (5%)
  starting transfers between devices  24 us (4%)
  between operations  14.1 us (3%)
  other arithmetic  7.75 us (1%)
    all_to_all x1, blocking collectives, local(): lax.all_to_all(first_spectra, 'ctx', split_axis=1, concat_axis=2, tiled=T...  98.2 us
    all_to_all x1, waiting for transfers between devices, swapped_in(): return jnp.concatenate(lax.all_to_all(sent, axis, 0, 0), axis=dim)  95.7 us
    reduce_scatter x1, waiting for transfers between devices, local(): lax.psum_scatter(partial_terms, 'ch', scatter_dimension=1, tiled=True)  94.5 us
    all_to_all x1, waiting for transfers between devices, local(): lax.all_to_all(halfway, 'ctx', split_axis=2, concat_axis=1, tiled=True)  48.8 us
    dot_general x8, matrix products, inner_product(): return jnp.einsum('kn,fnc->fkc', table, values, precision=highest_mode)  44.5 us
    all_to_all x1, waiting for transfers between devices, local(): lax.all_to_all(signal, 'ctx', split_axis=1, concat_axis=0, tiled=True)  26.9 us
    dot_general x1, matrix products, local(): jnp.einsum('kn,nbc->kbc', outer_cos, block_part, precision=highest_mode)  20.1 us
    all_to_all x1, blocking collectives, local(): lax.all_to_all(positions.astype(jnp.bfloat16), 'ctx', split_axis=0, conca...  16 us
  transfers between devices with their start and end apart: 4, of which 4 were waited for; matrix products, arithmetic and copies ran while one was open for 0% of the time, Pallas kernels for 0%

profile of v1, /device:TPU:40, one launch (start us, length us, event | category | flops | bytes accessed | tf_op | source)
XLA Modules:
  0.0 537.7 jit_solution(5009540644270513253)
XLA Ops:
  6.5 1.3 copy.63
  7.8 2.5 stack.36
  10.4 7.7 %all-to-all-start = ((bf16[8,2048,128]{1,2,0:T(8,128)(2,1)}), bf16[8,2048,128]{1,2,0:T(8,128)(2,1)}, u32[]{:S(2)}, u32[]{:S(2)}) async-start(bf16[8,2048,128]{1,2,0:T(8,128)(2,1)} %stack.36), calls=%async_computation | async-start | bytes 8388608 | tf_op jit(solution)/shard_map/all_to_all | solution.py:13
  18.1 1.0 fusion.152
  19.1 95.7 %all-to-all-done = bf16[8,2048,128]{1,2,0:T(8,128)(2,1)} async-done(((bf16[8,2048,128]{1,2,0:T(8,128)(2,1)}), bf16[8,2048,128]{1,2,0:T(8,128)(2,1)}, u32[]{:S(2)}, u32[]{:S(2)}) %all-to-all-start) | async-done | bytes 4194336 | tf_op jit(solution)/shard_map/all_to_all | solution.py:13
  114.8 2.9 fusion.151
  117.8 0.2 pad_maximum_fusion.2
  118.0 0.9 copy.96
  118.9 2.1 copy.64
  120.9 8.8 %all-to-all-start.1 = ((f32[8,256,256]{2,0,1:T(8,128)}), f32[8,256,256]{2,0,1:T(8,128)S(1)}, u32[]{:S(2)}, u32[]{:S(2)}) async-start(f32[8,256,256]{2,0,1:T(8,128)} %copy.64), calls=%async_computation.1 | async-start | bytes 4194304 | tf_op jit(solution)/shard_map/all_to_all | solution.py:45
  129.8 0.2 fusion.96
  129.9 26.9 %all-to-all-done.1 = f32[8,256,256]{2,0,1:T(8,128)S(1)} async-done(((f32[8,256,256]{2,0,1:T(8,128)}), f32[8,256,256]{2,0,1:T(8,128)S(1)}, u32[]{:S(2)}, u32[]{:S(2)}) %all-to-all-start.1) | async-done | bytes 2097184 | tf_op jit(solution)/shard_map/all_to_all | solution.py:45
  156.8 5.8 %fusion.26 = f32[512,8,256]{2,0,1:T(8,128)S(1)} fusion(f32[32,8,8,256]{3,1,2,0:T(8,128)S(1)} %bitcast.130), kind=kOutput, calls=%fused_computation.34 | convolution fusion | flops 3223060480 | bytes 6291456 | tf_op jit(solution)/shard_map/kn,nbc->kbc/dot_general | solution.py:47
  162.6 20.1 %add_bitcast_fusion.1 = (f32[1,512,8,256]{3,1,2,0:T(8,128)S(1)}, f32[1,512,8,256]{3,1,2,0:T(8,128)S(1)}) fusion(f32[512,8,256]{2,0,1:T(8,128)S(1)} %fusion.26, f32[512,8]{0,1:T(8,128)S(1)} %get-tuple-element.16, f32[512,8]{0,1:T(8,128)S(1)} %get-tuple-element.15, f32[32,8,8,256]{3,1,2,0:T(8,128)S(1)} %bitcast.131), kind=kOutput, calls=%fused_computation.14 | convolution fusion | flops 3230400512 | bytes 14712832 | tf_op jit(solution)/shard_map/kn,nbc->kbc/dot_general | solution.py:46
  182.7 0.7 pad_maximum_fusion
  183.5 4.9 copy.69
  188.3 98.2 %all_to_all.71 = f32[2,512,8,256]{3,2,0,1:T(8,128)S(1)} all-to-all(f32[2,512,8,256]{3,2,0,1:T(8,128)S(1)} %copy.69), channel_id=1, replica_groups=mesh['ctx'=32,'ch'=8] {'ctx'}, dimensions={1} | all-to-all | bytes 16777216 | tf_op jit(solution)/shard_map/all_to_all | solution.py:58
  286.5 0.7 copy.70
  287.2 1.0 fusion.145
  288.1 7.9 %fusion.2 = f32[16,256,256]{2,1,0:T(8,128)S(1)} fusion(f32[1,16,32,8,256]{4,3,1,2,0:T(8,128)S(1)} %get-tuple-element.10), kind=kOutput, calls=%fused_computation.4 | convolution fusion | flops 3222142976 | bytes 8388608 | tf_op jit(solution)/shard_map/kn,fnc->fkc/dot_general | solution.py:56
  296.1 8.4 %fusion = f32[16,256,256]{2,1,0:T(8,128)S(1)} fusion(f32[1,16,32,8,256]{4,3,1,2,0:T(8,128)S(1)} %get-tuple-element.10), kind=kOutput, calls=%fused_computation.2 | convolution fusion | flops 3222142976 | bytes 8388608 | tf_op jit(solution)/shard_map/kn,fnc->fkc/dot_general | solution.py:56
  304.5 8.3 %add_bitcast_fusion = f32[1,16,256,256]{2,3,1,0:T(8,128)S(1)} fusion(f32[16,256,256]{2,1,0:T(8,128)S(1)} %fusion.2, f32[1,16,32,8,256]{4,3,1,2,0:T(8,128)S(1)} %get-tuple-element.9), kind=kOutput, calls=%fused_computation.12 | convolution fusion | flops 3223191552 | bytes 12582912 | tf_op jit(solution)/shard_map/kn,fnc->fkc/dot_general | solution.py:56
  312.8 8.3 %subtract_bitcast_fusion = f32[1,16,256,256]{2,3,1,0:T(8,128)S(1)} fusion(f32[16,256,256]{2,1,0:T(8,128)S(1)} %fusion, f32[1,16,32,8,256]{4,3,1,2,0:T(8,128)S(1)} %get-tuple-element.9), kind=kOutput, calls=%fused_computation.11 | convolution fusion | flops 3223191552 | bytes 12582912 | tf_op jit(solution)/shard_map/kn,fnc->fkc/dot_general | solution.py:56
  321.1 0.7 multiply_subtract_fusion
  321.8 2.8 fusion.20
  324.6 3.0 fusion.18
  327.7 2.9 subtract_bitcast_fusion.2
  330.5 2.9 add_bitcast_fusion.2
  333.4 2.3 pad_maximum_fusion.1
  335.7 5.5 %copy.77 = f32[2,16,256,128]{3,1,0,2:T(8,128)} copy(f32[2,16,256,128]{2,3,1,0:T(8,128)} %pad_maximum_fusion.1) | data formatting | bytes 8388608 | tf_op jit(solution)/shard_map/stack | solution.py:71
  341.2 7.2 %all-to-all-start.3 = ((f32[2,16,256,128]{3,1,0,2:T(8,128)}), f32[2,16,256,128]{3,1,0,2:T(8,128)}, u32[]{:S(2)}, u32[]{:S(2)}) async-start(f32[2,16,256,128]{3,1,0,2:T(8,128)} %copy.77), calls=%async_computation.3 | async-start | bytes 8388608 | tf_op jit(solution)/shard_map/all_to_all | solution.py:72
  348.4 0.3 reduce-scatter.2.cloned.1.call-start
  348.7 0.1 copy.80
  348.8 0.1 copy.82
  349.0 48.8 %all-to-all-done.3 = f32[2,16,256,128]{3,1,0,2:T(8,128)} async-done(((f32[2,16,256,128]{3,1,0,2:T(8,128)}), f32[2,16,256,128]{3,1,0,2:T(8,128)}, u32[]{:S(2)}, u32[]{:S(2)}) %all-to-all-start.3) | async-done | bytes 4194336 | tf_op jit(solution)/shard_map/all_to_all | solution.py:72
  397.8 4.6 copy.138
  402.4 0.4 fusion.146
  402.8 0.3 copy.79
  403.1 0.3 copy.81
  403.3 1.6 fusion.16
  405.0 3.9 fusion.30
  408.9 4.0 fusion.46
  412.9 0.3 copy.85
  413.3 16.0 %all_to_all.72 = bf16[256,8,128]{2,1,0:T(8,128)(2,1)S(1)} all-to-all(bf16[256,8,128]{2,1,0:T(8,128)(2,1)S(1)} %copy.85), channel_id=1, replica_groups=mesh['ctx'=32,'ch'=8] {'ctx'}, dimensions={0} | all-to-all | bytes 1048576 | tf_op jit(solution)/shard_map/all_to_all | solution.py:81
  429.2 0.1 copy.86
  429.3 4.5 fusion.153
  433.8 94.5 %reduce-scatter.2.cloned.1.call-done = f32[2048,128]{1,0:T(8,128)} async-done(((f32[2048,1024]{1,0:T(8,128)}), f32[2048,128]{1,0:T(8,128)}) %reduce-scatter.2.cloned.1.call-update) | async-done | bytes 1048592 | tf_op jit(solution)/shard_map/reduce_scatter | solution.py:89
  528.3 2.1 convert_element_type.49
  (10 shorter events, 0.0 us)
Async XLA Ops:
  6.5 422.8 %copy-start = (bf16[128,1024]{1,0:T(8,128)(2,1)S(1)}, bf16[128,1024]{1,0:T(8,128)(2,1)}, u32[]{:S(2)}) copy-start(bf16[128,1024]{1,0:T(8,128)(2,1)} %param.9) | copy-start | bytes 786436
  10.4 7.7 %copy-start.2 = (f32[2048,24]{0,1:T(8,128)S(1)}, f32[2048,24]{0,1:T(8,128)}, u32[]{:S(2)}) copy-start(f32[2048,24]{0,1:T(8,128)} %param.7) | copy-start | bytes 589828
  10.4 7.7 %copy-start.3 = (f32[24,128]{1,0:T(8,128)S(1)}, f32[24,128]{1,0:T(8,128)}, u32[]{:S(2)}) copy-start(f32[24,128]{1,0:T(8,128)} %param.8) | copy-start | bytes 36868
  10.4 104.5 %copy-start.1 = (bf16[1024,128]{1,0:T(8,128)(2,1)S(1)}, bf16[1024,128]{1,0:T(8,128)(2,1)}, u32[]{:S(2)}) copy-start(bf16[1024,128]{1,0:T(8,128)(2,1)} %param.6) | copy-start | bytes 786436
  10.4 104.5 %all-to-all-start = ((bf16[8,2048,128]{1,2,0:T(8,128)(2,1)}), bf16[8,2048,128]{1,2,0:T(8,128)(2,1)}, u32[]{:S(2)}, u32[]{:S(2)}) async-start(bf16[8,2048,128]{1,2,0:T(8,128)(2,1)} %stack.36), calls=%async_computation | async-start | bytes 8388608 | tf_op jit(solution)/shard_map/all_to_all | solution.py:13
  120.9 35.9 %all-to-all-start.1 = ((f32[8,256,256]{2,0,1:T(8,128)}), f32[8,256,256]{2,0,1:T(8,128)S(1)}, u32[]{:S(2)}, u32[]{:S(2)}) async-start(f32[8,256,256]{2,0,1:T(8,128)} %copy.64), calls=%async_computation.1 | async-start | bytes 4194304 | tf_op jit(solution)/shard_map/all_to_all | solution.py:45
  341.2 56.5 %all-to-all-start.3 = ((f32[2,16,256,128]{3,1,0,2:T(8,128)}), f32[2,16,256,128]{3,1,0,2:T(8,128)}, u32[]{:S(2)}, u32[]{:S(2)}) async-start(f32[2,16,256,128]{3,1,0,2:T(8,128)} %copy.77), calls=%async_computation.3 | async-start | bytes 8388608 | tf_op jit(solution)/shard_map/all_to_all | solution.py:72
  348.4 179.9 %reduce-scatter.2.cloned.1.call-start = ((), (), s32[]{:S(2)}) async-start(), calls=%async_computation.6 | async-start | bytes 9437184 | tf_op jit(solution)/shard_map/reduce_scatter | solution.py:89
Sparse Core Ops, SparseCore 0:
  434.0 94.2 reduce-scatter.1
